TPU v7x, 512 devices: a whole 4x8x8 slice. The times are simulated.
512 devices in a mesh: seq: 64 (over z, x, core), head: 8 (over y).
Axes of the slice: x: 4, y: 8, z: 8, core: 2. Of those that a mesh axis runs over, the one named last changes fastest.
Arguments:
- loaded: bfloat16 [8192, 2048], P('seq', 'head'), may hold values from -6 to 6
- out_grad: bfloat16 [8192, 2048], P('seq', 'head'), may hold values from -6 to 6
- w_query: bfloat16 [2048, 2048], P(None, 'head'), may hold values from -0.125 to 0.125
- w_key: bfloat16 [2048, 2048], P(None, 'head'), may hold values from -0.125 to 0.125
- w_value: bfloat16 [2048, 2048], P(None, 'head'), may hold values from -0.125 to 0.125
- w_beta: bfloat16 [2048, 16], P(None, 'head'), may hold values from -0.125 to 0.125
- beta_max: float32 [16], P('head'), may hold values from 0.015625 to 1
- out_gain: float32 [128], replicated, may hold values from 0.1 to 1.9
- clip_lengths: int32 [16], replicated, may hold values from 1 to 2048, 8192 in all
- delay_offsets: int32 [4], replicated, may hold values from 0 to 3, each once
- block_order: int32 [64, 64], P('seq'), may hold values from 0 to 63, each once within a row
Outputs:
- head_out: bfloat16 [8192, 2048], P('seq', 'head')
- input_grad: bfloat16 [8192, 2048], P('seq', 'head')
Inputs may be any that keep to these rules, and one draw needn't show every extreme that they name: `clip_lengths`: the clip lengths sum to 8192; the longest is exactly 2048. `delay_offsets`: each codebook has a different delay. `block_order`: each row is a permutation of 0 to 63.
All inputs are finite; a program needn't handle non-finite values.
Results may differ from a plain program's by a relative error of at most 0.022.
Values may be sent and summed in bfloat16 or wider, within the bound.
A program may use at most 128 MiB of HBM per device.

v0:
```python
import jax
import jax.numpy as jnp
from jax import lax
from jax.sharding import PartitionSpec as P

SPAN = 128
EPSILON = 1e-06
HIGHEST = lax.Precision.HIGHEST


def from_behind(x, axis, by):
    count = lax.axis_size(axis)
    pairs = [(i, i + by) for i in range(count) if 0 <= i + by < count]
    return lax.ppermute(x, axis, pairs)


def prefix(x, axis, join, neutral):
    place = lax.axis_index(axis)
    gathered = jax.tree.map(
        lambda a, kind: lax.all_gather(a.astype(kind), axis), x, (jnp.bfloat16, jnp.bfloat16)
    )
    state = jax.tree.map(lambda a, e: jnp.zeros_like(a) + jnp.asarray(e, a.dtype), x, neutral)

    def one(turn, state):
        return join(
            state,
            jax.tree.map(
                lambda a, own: lax.dynamic_index_in_dim(a, turn, 0, False).astype(own.dtype),
                gathered,
                x,
            ),
        )

    return lax.fori_loop(0, place, one, state)


def prefix_2(x, axis, combine, identity):
    count, here = (lax.axis_size(axis), lax.axis_index(axis))
    everything = jax.tree.map(
        lambda part, kind: lax.all_gather(part.astype(kind), axis),
        x,
        jax.tree.map(lambda a: jnp.bfloat16 if a.dtype == jnp.float32 else a.dtype, x),
    )
    start = jax.tree.map(
        lambda part, zero: jnp.broadcast_to(jnp.asarray(zero, part.dtype), part.shape), x, identity
    )

    def turn(k, before):
        at = count - 1 - k
        reached = at > here
        new = combine(
            before, jax.tree.map(lambda part, own: part[at].astype(own.dtype), everything, x)
        )
        return jax.tree.map(lambda a, b: jnp.where(reached, a, b), new, before)

    return lax.fori_loop(0, count, turn, start)


def clip_start(clip_lengths, positions):
    clip_ends = jnp.cumsum(clip_lengths)
    finished = clip_ends[None, :] <= positions[:, None]
    return jnp.sum(jnp.where(finished, clip_lengths[None, :], 0), axis=1)


def column_delays(delay_offsets, columns, group_width):
    codebook = columns // group_width
    matches = codebook[:, None] == jnp.arange(delay_offsets.shape[0], dtype=jnp.int32)[None, :]
    return jnp.sum(jnp.where(matches, delay_offsets[None, :], 0), axis=1)


def prepare(q_raw, k_raw, logit, rate_cap):
    query_rows = q_raw / jnp.sqrt(jnp.sum(q_raw * q_raw, axis=-1, keepdims=True) + EPSILON)
    key_rows = k_raw / jnp.sqrt(jnp.sum(k_raw * k_raw, axis=-1, keepdims=True) + EPSILON)
    beta_rate = rate_cap * jax.nn.sigmoid(logit[:, 0])
    return (query_rows, key_rows, beta_rate)


def span_terms(key_rows, value_rows, beta_rate, clip_begin, span_first):
    span_len = key_rows.shape[0]
    key_width = key_rows.shape[1]
    same_clip = (clip_begin[:, None] == clip_begin[None, :]).astype(jnp.float32)
    gram = beta_rate[:, None] * jnp.dot(key_rows, key_rows.T, precision=HIGHEST) * same_clip
    system = jnp.eye(span_len, dtype=jnp.float32) + jnp.tril(gram, -1)
    stacked = beta_rate[:, None] * jnp.concatenate([key_rows, value_rows], axis=1)
    solved = jax.scipy.linalg.solve_triangular(system, stacked, lower=True, unit_diagonal=True)
    carried = (clip_begin < span_first).astype(jnp.float32)
    final_mask = (clip_begin == clip_begin[-1]).astype(jnp.float32)
    return (solved[:, :key_width], solved[:, key_width:], carried, final_mask, same_clip)


def span_output(state_in, pieces):
    query_rows, key_rows, value_rows, beta_rate, clip_begin, span_first = pieces
    key_part, value_part, carried, final_mask, same_clip = span_terms(
        key_rows, value_rows, beta_rate, clip_begin, span_first
    )
    refreshed = value_part - carried[:, None] * jnp.dot(key_part, state_in, precision=HIGHEST)
    scores = jnp.tril(jnp.dot(query_rows, key_rows.T, precision=HIGHEST)) * same_clip
    outputs = carried[:, None] * jnp.dot(query_rows, state_in, precision=HIGHEST) + jnp.dot(
        scores, refreshed, precision=HIGHEST
    )
    state_out = carried[-1] * state_in + jnp.dot(
        key_rows.T, final_mask[:, None] * refreshed, precision=HIGHEST
    )
    return (state_out, outputs)


def affine_step(affine, pieces):
    key_rows, value_rows, beta_rate, clip_begin, span_first = pieces
    key_part, value_part, carried, final_mask, same_clip = span_terms(
        key_rows, value_rows, beta_rate, clip_begin, span_first
    )
    widened = jnp.concatenate(
        [jnp.zeros((key_rows.shape[0], key_rows.shape[1]), jnp.float32), value_part], axis=1
    )
    refreshed = widened - carried[:, None] * jnp.dot(key_part, affine, precision=HIGHEST)
    return (
        carried[-1] * affine
        + jnp.dot(key_rows.T, final_mask[:, None] * refreshed, precision=HIGHEST),
        None,
    )


def run_head(q_raw, k_raw, v_raw, logit, rate_cap, out_gain, clip_begin, positions, state_in):
    query_rows, key_rows, beta_rate = prepare(q_raw, k_raw, logit, rate_cap)
    span_count = q_raw.shape[0] // SPAN
    pieces = (
        query_rows.reshape(span_count, SPAN, -1),
        key_rows.reshape(span_count, SPAN, -1),
        v_raw.reshape(span_count, SPAN, -1),
        beta_rate.reshape(span_count, SPAN),
        clip_begin.reshape(span_count, SPAN),
        positions.reshape(span_count, SPAN)[:, 0],
    )
    state_out, outputs = lax.scan(span_output, state_in, pieces)
    raw_out = outputs.reshape(-1, outputs.shape[-1])
    normed = (
        raw_out
        / jnp.sqrt(jnp.mean(raw_out * raw_out, axis=-1, keepdims=True) + EPSILON)
        * out_gain[None, :]
    )
    return (normed, state_out)


def compose(before_map, after_map):
    return (
        jnp.matmul(after_map[0], before_map[0], precision=HIGHEST),
        jnp.matmul(after_map[0], before_map[1], precision=HIGHEST) + after_map[1],
    )


def back_product(gradient, weight):
    return lax.dot_general(
        gradient, weight, (((1,), (1,)), ((), ())), preferred_element_type=jnp.float32
    )


def split_heads(matrix, heads_local):
    return matrix.reshape(matrix.shape[0], heads_local, -1).transpose(1, 0, 2)


def join_heads(stacked):
    return stacked.transpose(1, 0, 2).reshape(stacked.shape[1], -1)


def on_device(
    loaded,
    out_grad,
    w_query,
    w_key,
    w_value,
    w_beta,
    beta_max,
    out_gain,
    clip_lengths,
    delay_offsets,
    block_order,
):
    sources = lax.axis_size("seq")
    frames = loaded.shape[0]
    local_width = loaded.shape[1]
    block_rows = frames // sources
    received = lax.all_to_all(
        loaded.reshape(sources, block_rows, local_width),
        "seq",
        split_axis=0,
        concat_axis=0,
        tiled=True,
    )
    inverse = jnp.argsort(block_order[0])
    arranged = jnp.take(received, inverse, axis=0).reshape(frames, local_width)
    positions = lax.axis_index("seq") * frames + jnp.arange(frames, dtype=jnp.int32)
    clip_begin = clip_start(clip_lengths, positions)
    codebooks = delay_offsets.shape[0]
    delay_reach = codebooks - 1
    full_width = local_width * lax.axis_size("head")
    columns = lax.axis_index("head") * local_width + jnp.arange(local_width, dtype=jnp.int32)
    col_delay = column_delays(delay_offsets, columns, full_width // codebooks)
    earlier = from_behind(arranged[frames - delay_reach :], "seq", 1)
    extended = jnp.concatenate([earlier, arranged], axis=0)
    delayed = jnp.zeros((frames, local_width), jnp.bfloat16)
    for shift_by in range(codebooks):
        shifted = extended[delay_reach - shift_by : delay_reach - shift_by + frames]
        inside = positions - shift_by >= clip_begin
        delayed = jnp.where((col_delay[None, :] == shift_by) & inside[:, None], shifted, delayed)
    heads_local = w_beta.shape[1]
    key_width = w_query.shape[1] // heads_local
    value_width = w_value.shape[1] // heads_local
    empty = (
        jnp.zeros((frames, w_query.shape[1]), jnp.float32),
        jnp.zeros((frames, w_key.shape[1]), jnp.float32),
        jnp.zeros((frames, w_value.shape[1]), jnp.float32),
        jnp.zeros((frames, heads_local), jnp.float32),
    )
    feature_part = lax.all_gather(delayed, "head", axis=1, tiled=True)
    results = []
    for running, weight in zip(empty, (w_query, w_key, w_value, w_beta)):
        results.append(jnp.dot(feature_part, weight, preferred_element_type=jnp.float32))
    q_flat, k_flat, v_flat, logit_flat = tuple(results)
    q_heads = split_heads(q_flat, heads_local)
    k_heads = split_heads(k_flat, heads_local)
    v_heads = split_heads(v_flat, heads_local)
    logit_heads = split_heads(logit_flat, heads_local)
    span_count = frames // SPAN
    start_affine = jnp.concatenate(
        [jnp.eye(key_width, dtype=jnp.float32), jnp.zeros((key_width, value_width), jnp.float32)],
        axis=1,
    )

    def head_affine(q_one, k_one, v_one, logit_one, rate_cap):
        query_rows, key_rows, beta_rate = prepare(q_one, k_one, logit_one, rate_cap)
        map_pieces = (
            key_rows.reshape(span_count, SPAN, -1),
            v_one.reshape(span_count, SPAN, -1),
            beta_rate.reshape(span_count, SPAN),
            clip_begin.reshape(span_count, SPAN),
            positions.reshape(span_count, SPAN)[:, 0],
        )
        affine, _ = lax.scan(affine_step, start_affine, map_pieces)
        return affine

    affine = jax.vmap(head_affine)(q_heads, k_heads, v_heads, logit_heads, beta_max)
    transition = affine[:, :, :key_width]
    offset_map = affine[:, :, key_width:]
    identity = (
        jnp.broadcast_to(
            jnp.eye(key_width, dtype=jnp.float32), (heads_local, key_width, key_width)
        ),
        jnp.zeros((heads_local, key_width, value_width), jnp.float32),
    )
    _, state_in = prefix((transition, offset_map), "seq", compose, identity)

    def forward(query_in, key_in, value_in, logit_in, state_start):

        def one_head(q_one, k_one, v_one, logit_one, rate_cap, state_one):
            return run_head(
                q_one, k_one, v_one, logit_one, rate_cap, out_gain, clip_begin, positions, state_one
            )

        return jax.vmap(one_head)(query_in, key_in, value_in, logit_in, beta_max, state_start)

    (normed, state_out), pullback = jax.vjp(
        forward, q_heads, k_heads, v_heads, logit_heads, state_in
    )
    head_out = join_heads(normed).astype(jnp.bfloat16)
    cotangent = split_heads(out_grad, heads_local).astype(jnp.float32)
    first_pass = pullback((cotangent, jnp.zeros_like(state_out)))
    _, state_grad = prefix_2(
        (jnp.swapaxes(transition, 1, 2), first_pass[4]), "seq", compose, identity
    )
    second_pass = pullback((jnp.zeros_like(normed), state_grad))
    gradients = [
        join_heads(first_pass[index] + second_pass[index]).astype(jnp.bfloat16)
        for index in range(4)
    ]
    partial_sum = back_product(gradients[0], w_query) + back_product(gradients[1], w_key)
    partial_sum = (
        partial_sum + back_product(gradients[2], w_value) + back_product(gradients[3], w_beta)
    )
    summed = lax.psum_scatter(
        partial_sum.astype(jnp.bfloat16), "head", scatter_dimension=1, tiled=True
    )
    following = from_behind(summed[:delay_reach], "seq", -1)
    extended_grad = jnp.concatenate([summed, following], axis=0)
    input_grad = jnp.zeros((frames, local_width), jnp.bfloat16)
    for shift_by in range(codebooks):
        ahead = extended_grad[shift_by : shift_by + frames]
        inside = clip_start(clip_lengths, positions + shift_by) <= positions
        input_grad = jnp.where(
            (col_delay[None, :] == shift_by) & inside[:, None], ahead, input_grad
        )
    return (head_out, input_grad)


def solution(mesh):
    return jax.shard_map(
        on_device,
        mesh=mesh,
        in_specs=(
            P("seq", "head"),
            P("seq", "head"),
            P(None, "head"),
            P(None, "head"),
            P(None, "head"),
            P(None, "head"),
            P("head"),
            P(),
            P(),
            P(),
            P("seq", None),
        ),
        out_specs=(P("seq", "head"), P("seq", "head")),
        check_vma=False,
    )
```

profile of v0, /device:TPU:1, one launch (start us, length us, event | category | flops | bytes accessed | tf_op | source)
XLA Modules:
  0.0 574.0 jit_solution(4794235348666533601)
XLA Ops:
  7.2 1.6 reshape.670
  8.9 14.8 %all-to-all-start = ((bf16[64,2,256]{2,1,0:T(2,128)(2,1)}), bf16[64,2,256]{2,1,0:T(2,128)(2,1)S(1)}, u32[]{:S(2)}, u32[]{:S(2)}) async-start(bf16[64,2,256]{2,1,0:T(2,128)(2,1)} %reshape.670), calls=%async_computation | async-start | bytes 131072 | tf_op jit(solution)/shard_map/all_to_all | solution.py:182
  23.8 2.7 sort.17
  27.4 1.3 select_reduce_fusion.2
  30.8 1.9 fusion.106
  35.1 3.5 collective-permute-start
  39.5 21.1 %all_gather.27 = bf16[128,2048]{1,0:T(8,128)(2,1)S(1)} all-gather(bf16[128,256]{1,0:T(8,128)(2,1)S(1)} %and_select_fusion.7), channel_id=1, replica_groups=mesh['seq'=64,'head'=8] {'head'}, dimensions={1}, use_global_device_ids=true | all-gather | bytes 589824 | tf_op jit(solution)/shard_map/all_gather | solution.py:214
  60.7 1.8 multiply_reduce_fusion.10
  64.9 19.7 %custom-call.10 = f32[2,1,128,128]{2,3,1,0:T(8,128)S(1)} custom-call(f32[2,1,128,128]{3,2,1,0:T(8,128)S(1)} %add_bitcast_fusion), custom_call_target="InvertDiagBlocksLowerTriangular" | custom-call | tf_op jit(solution)/shard_map/vmap()/while/body/eval_jaxpr/jit(_solve_triangular)/triangular_solve/custom-call.1 | solution.py:85
  90.5 1.6 copy.156
  94.4 87.9 %all-gather.9.cloned.1.call-done = bf16[128,128,128]{2,1,0:T(8,128)(2,1)} async-done(((bf16[2,128,128]{2,1,0:T(8,128)(2,1)}), bf16[128,128,128]{2,1,0:T(8,128)(2,1)}) %all-gather.9.cloned.1.call-update) | async-done | bytes 4194320 | tf_op jit(solution)/shard_map/all_gather | solution.py:20
  182.3 85.9 %all-gather.11.cloned.1.call-done = bf16[128,128,128]{2,1,0:T(8,128)(2,1)} async-done(((bf16[2,128,128]{2,1,0:T(8,128)(2,1)}), bf16[128,128,128]{2,1,0:T(8,128)(2,1)}) %all-gather.11.cloned.1.call-update) | async-done | bytes 4194320 | tf_op jit(solution)/shard_map/all_gather | solution.py:20
  268.3 1.1 while.25
  275.7 1.1 fusion.63
  278.9 74.5 %all-gather.13.cloned.1.call-done = bf16[128,128,128]{2,1,0:T(8,128)(2,1)} async-done(((bf16[2,128,128]{2,1,0:T(8,128)(2,1)}), bf16[128,128,128]{2,1,0:T(8,128)(2,1)}) %all-gather.13.cloned.1.call-update) | async-done | bytes 4194320 | tf_op jit(solution)/shard_map/all_gather | solution.py:40
  353.4 86.0 %all-gather.15.cloned.1.call-done = bf16[128,128,128]{2,1,0:T(8,128)(2,1)} async-done(((bf16[2,128,128]{2,1,0:T(8,128)(2,1)}), bf16[128,128,128]{2,1,0:T(8,128)(2,1)}) %all-gather.15.cloned.1.call-update) | async-done | bytes 4194320 | tf_op jit(solution)/shard_map/all_gather | solution.py:40
  439.4 73.4 %while.26 = (s32[]{:T(128)}, f32[2,128,128]{2,1,0:T(8,128)S(1)}, s32[]{:T(128)}, bf16[64,2,128,128]{3,2,1,0:T(8,128)(2,1)}, bf16[64,2,128,128]{3,2,1,0:T(8,128)(...) while((s32[]{:T(128)}, f32[2,128,128]{2,1,0:T(8,128)S(1)}, s32[]{:T(128)}, ...), condition=%wide.region_16.19_spmd.clone, body=%wide.region_15.18_spmd.clone.sunk | while | flops 50495496 | bytes 789149 | solution.py:56
  439.4 1.1 fusion.165
  441.7 1.1 fusion.165
  442.9 1.1 fusion.165
  445.2 1.1 fusion.165
  446.3 1.1 fusion.165
  449.8 1.1 fusion.165
  453.2 1.1 fusion.165
  456.7 1.1 fusion.165
  460.1 1.1 fusion.165
  463.5 1.1 fusion.165
  467.0 1.1 fusion.165
  470.4 1.1 fusion.165
  473.9 1.1 fusion.165
  477.3 1.1 fusion.165
  480.8 1.1 fusion.165
  484.2 1.1 fusion.165
  487.7 1.1 fusion.165
  491.1 1.1 fusion.165
  494.5 1.1 fusion.165
  498.0 1.1 fusion.165
  501.4 1.1 fusion.165
  504.9 1.1 fusion.165
  508.3 1.1 fusion.165
  511.8 1.1 fusion.165
  513.3 1.4 convolution_add_fusion.8
  516.7 1.7 multiply_reduce_fusion.1
  522.9 1.2 fusion.11
  525.2 30.2 %reduce-scatter.2.cloned.1.call-done = bf16[128,256]{1,0:T(8,128)(2,1)} async-done(((bf16[128,2048]{1,0:T(8,128)(2,1)}), bf16[128,256]{1,0:T(8,128)(2,1)}) %reduce-scatter.2.cloned.1.call-update) | async-done | bytes 65552 | tf_op jit(solution)/shard_map/reduce_scatter | solution.py:279
  556.0 7.5 %collective-permute-start.1 = (bf16[3,256]{1,0:T(4,128)(2,1)S(1)}, bf16[3,256]{1,0:T(4,128)(2,1)S(1)}, u32[]{:S(2)}, u32[]{:S(2)}) collective-permute-start(bf16[3,256]{1,0:T(4,128)(2,1)S(1)} %slice.115), channel_id=1, source_target_pairs={{8,0},{16,8},{24,16},{32,24},{40,32},{48,40},{56,48},{64,56},{72,6... | collective-permute-start | bytes 4616 | tf_op jit(solution)/shard_map/ppermute | solution.py:14
  564.4 1.5 collective-permute-done.1
  565.9 1.6 and_select_fusion.3
  (313 shorter events, 78.8 us)
Async XLA Ops:
  7.2 85.9 %copy-start = (bf16[2048,256]{1,0:T(8,128)(2,1)S(1)}, bf16[2048,256]{1,0:T(8,128)(2,1)}, u32[]{:S(2)}) copy-start(bf16[2048,256]{1,0:T(8,128)(2,1)} %param.23) | copy-start | bytes 3145732
  7.2 56.3 %copy-start.27 = (bf16[2048,2]{0,1:T(2,128)(2,1)S(1)}, bf16[2048,2]{0,1:T(2,128)(2,1)}, u32[]{:S(2)}) copy-start(bf16[2048,2]{0,1:T(2,128)(2,1)} %param.26) | copy-start | bytes 24580
  7.2 56.3 %copy-start.44 = (f32[2]{0:T(128)S(1)}, f32[2]{0:T(128)}, u32[]{:S(2)}) copy-start(f32[2]{0:T(128)} %param.27) | copy-start | bytes 28
  7.2 77.4 %copy-start.2 = (bf16[2048,256]{1,0:T(8,128)(2,1)S(1)}, bf16[2048,256]{1,0:T(8,128)(2,1)}, u32[]{:S(2)}) copy-start(bf16[2048,256]{1,0:T(8,128)(2,1)} %param.25) | copy-start | bytes 3145732
  8.9 25.4 %all-to-all-start = ((bf16[64,2,256]{2,1,0:T(2,128)(2,1)}), bf16[64,2,256]{2,1,0:T(2,128)(2,1)S(1)}, u32[]{:S(2)}, u32[]{:S(2)}) async-start(bf16[64,2,256]{2,1,0:T(2,128)(2,1)} %reshape.670), calls=%async_computation | async-start | bytes 131072 | tf_op jit(solution)/shard_map/all_to_all | solution.py:182
  23.7 158.6 %all-gather.9.cloned.1.call-start = ((), (), s32[]{:S(2)}) async-start(), calls=%async_computation.3 | async-start | bytes 4259840 | tf_op jit(solution)/shard_map/all_gather | solution.py:20
  30.7 33.6 %copy-start.31 = (pred[256]{0:T(512)(128)(4,1)}, pred[256]{0:T(512)(128)(4,1)S(1)}, u32[]{:S(2)}) copy-start(pred[256]{0:T(512)(128)(4,1)S(1)} %get-tuple-element.999) | copy-start | bytes 772
  30.7 33.6 %copy-start.33 = (pred[256]{0:T(512)(128)(4,1)}, pred[256]{0:T(512)(128)(4,1)S(1)}, u32[]{:S(2)}) copy-start(pred[256]{0:T(512)(128)(4,1)S(1)} %get-tuple-element.1000) | copy-start | bytes 772
  30.7 33.6 %copy-start.35 = (pred[256]{0:T(512)(128)(4,1)}, pred[256]{0:T(512)(128)(4,1)S(1)}, u32[]{:S(2)}) copy-start(pred[256]{0:T(512)(128)(4,1)S(1)} %get-tuple-element.1001) | copy-start | bytes 772
  30.7 33.6 %copy-start.37 = (pred[256]{0:T(512)(128)(4,1)}, pred[256]{0:T(512)(128)(4,1)S(1)}, u32[]{:S(2)}) copy-start(pred[256]{0:T(512)(128)(4,1)S(1)} %get-tuple-element.1002) | copy-start | bytes 772
  35.1 4.3 collective-permute-start
  39.5 52.6 %copy-start.16 = (bf16[128,256]{1,0:T(8,128)(2,1)S(1)}, bf16[128,256]{1,0:T(8,128)(2,1)}, u32[]{:S(2)}) copy-start(bf16[128,256]{1,0:T(8,128)(2,1)} %param.22) | copy-start | bytes 196612
  63.5 30.9 %copy-start.4 = (f32[2,128,128]{1,2,0:T(8,128)}, f32[2,128,128]{1,2,0:T(8,128)S(1)}, u32[]{:S(2)}) copy-start(f32[2,128,128]{1,2,0:T(8,128)S(1)} %bitcast_divide_fusion.4) | copy-start | bytes 393220
  84.6 8.4 %copy-start.29 = (f32[128]{0:T(128)S(1)}, f32[128]{0:T(128)}, u32[]{:S(2)}) copy-start(f32[128]{0:T(128)} %param.28) | copy-start | bytes 1540
  84.6 8.9 %copy-start.18 = (f32[2,128]{1,0:T(2,128)S(1)}, f32[2,128]{1,0:T(2,128)}, u32[]{:S(2)}) copy-start(f32[2,128]{1,0:T(2,128)} %copy-done.17) | copy-start | bytes 3076
  84.7 8.9 %copy-start.39 = (f32[128]{0:T(128)S(1)}, f32[128]{0:T(128)}, u32[]{:S(2)}) copy-start(f32[128]{0:T(128)} %get-tuple-element.1004) | copy-start | bytes 1540
  88.0 181.5 %copy-start.21 = (f32[128]{0:T(128)S(1)}, f32[128]{0:T(128)}, u32[]{:S(2)}) copy-start(f32[128]{0:T(128)} %copy-done.20) | copy-start | bytes 1540
  89.7 178.6 %all-gather.11.cloned.1.call-start = ((), (), s32[]{:S(2)}) async-start(), calls=%async_computation.4 | async-start | bytes 4259840 | tf_op jit(solution)/shard_map/all_gather | solution.py:20
  90.4 263.0 %all-gather.13.cloned.1.call-start = ((), (), s32[]{:S(2)}) async-start(), calls=%async_computation.5 | async-start | bytes 4259840 | tf_op jit(solution)/shard_map/all_gather | solution.py:40
  92.0 347.4 %all-gather.15.cloned.1.call-start = ((), (), s32[]{:S(2)}) async-start(), calls=%async_computation.6 | async-start | bytes 4259840 | tf_op jit(solution)/shard_map/all_gather | solution.py:40
  94.4 179.9 %copy-start.15 = (f32[2,128,128]{2,1,0:T(8,128)}, f32[2,128,128]{2,1,0:T(8,128)S(1)}, u32[]{:S(2)}) copy-start(f32[2,128,128]{2,1,0:T(8,128)S(1)} %fusion.25) | copy-start | bytes 393220
  268.2 6.6 %copy-start.19 = (f32[2,128]{1,0:T(2,128)S(1)}, f32[2,128]{1,0:T(2,128)}, u32[]{:S(2)}) copy-start(f32[2,128]{1,0:T(2,128)} %copy-done.17) | copy-start | bytes 3076
  269.4 6.3 %copy-start.40 = (f32[128]{0:T(128)S(1)}, f32[128]{0:T(128)}, u32[]{:S(2)}) copy-start(f32[128]{0:T(128)} %get-tuple-element.1004) | copy-start | bytes 1540
  272.7 282.6 %reduce-scatter.2.cloned.1.call-start = ((), (), s32[]{:S(2)}) async-start(), calls=%async_computation.2 | async-start | bytes 589824 | tf_op jit(solution)/shard_map/reduce_scatter | solution.py:279
  274.3 4.0 copy-start.7
  276.8 237.9 %copy-start.22 = (f32[128]{0:T(128)S(1)}, f32[128]{0:T(128)}, u32[]{:S(2)}) copy-start(f32[128]{0:T(128)} %copy-done.20) | copy-start | bytes 1540
  278.4 238.3 %copy-start.24 = (f32[2,128]{1,0:T(2,128)S(1)}, f32[2,128]{1,0:T(2,128)}, u32[]{:S(2)}) copy-start(f32[2,128]{1,0:T(2,128)} %copy-done.23) | copy-start | bytes 3076
  512.9 5.9 %copy-start.8 = (f32[2,128,128]{2,1,0:T(8,128)S(1)}, f32[2,128,128]{2,1,0:T(8,128)}, u32[]{:S(2)}) copy-start(f32[2,128,128]{2,1,0:T(8,128)} %copy-done.7) | copy-start | bytes 393220
  512.9 5.9 %copy-start.9 = (f32[2,128,128]{1,2,0:T(8,128)S(1)}, f32[2,128,128]{1,2,0:T(8,128)}, u32[]{:S(2)}) copy-start(f32[2,128,128]{1,2,0:T(8,128)} %fusion.63) | copy-start | bytes 393220
  512.9 6.2 %copy-start.11 = (f32[2,128,128]{2,1,0:T(8,128)S(1)}, f32[2,128,128]{2,1,0:T(8,128)}, u32[]{:S(2)}) copy-start(f32[2,128,128]{2,1,0:T(8,128)} %copy-done.10) | copy-start | bytes 393220
  512.9 6.5 %copy-start.12 = (f32[2,128,128]{1,2,0:T(8,128)S(1)}, f32[2,128,128]{1,2,0:T(8,128)}, u32[]{:S(2)}) copy-start(f32[2,128,128]{1,2,0:T(8,128)} %fusion.32) | copy-start | bytes 393220
  512.9 6.5 %copy-start.14 = (f32[2,128,128]{2,1,0:T(8,128)S(1)}, f32[2,128,128]{2,1,0:T(8,128)}, u32[]{:S(2)}) copy-start(f32[2,128,128]{2,1,0:T(8,128)} %copy-done.13) | copy-start | bytes 393220
  513.3 8.0 %copy-start.43 = (f32[2,128]{1,0:T(2,128)S(1)}, f32[2,128]{1,0:T(2,128)}, u32[]{:S(2)}) copy-start(f32[2,128]{1,0:T(2,128)} %get-tuple-element.988) | copy-start | bytes 3076
  515.2 6.5 %copy-start.26 = (f32[2,128]{1,0:T(2,128)S(1)}, f32[2,128]{1,0:T(2,128)}, u32[]{:S(2)}) copy-start(f32[2,128]{1,0:T(2,128)} %copy-done.25) | copy-start | bytes 3076
  515.8 6.0 %copy-start.1 = (bf16[2048,256]{1,0:T(8,128)(2,1)S(1)}, bf16[2048,256]{1,0:T(8,128)(2,1)}, u32[]{:S(2)}) copy-start(bf16[2048,256]{1,0:T(8,128)(2,1)} %param.24) | copy-start | bytes 3145732
  518.7 3.6 copy-start.3
  520.8 2.1 copy-start.28
  520.8 2.1 copy-start.42
  521.8 2.4 copy-start.48
  521.8 2.4 copy-start.47
  521.8 2.4 copy-start.46
  521.8 2.4 copy-start.30
  521.8 44.1 %copy-start.32 = (pred[256]{0:T(512)(128)(4,1)S(1)}, pred[256]{0:T(512)(128)(4,1)}, u32[]{:S(2)}) copy-start(pred[256]{0:T(512)(128)(4,1)} %copy-done.31) | copy-start | bytes 772
  521.8 44.1 %copy-start.34 = (pred[256]{0:T(512)(128)(4,1)S(1)}, pred[256]{0:T(512)(128)(4,1)}, u32[]{:S(2)}) copy-start(pred[256]{0:T(512)(128)(4,1)} %copy-done.33) | copy-start | bytes 772
  521.8 44.0 %copy-start.36 = (pred[256]{0:T(512)(128)(4,1)S(1)}, pred[256]{0:T(512)(128)(4,1)}, u32[]{:S(2)}) copy-start(pred[256]{0:T(512)(128)(4,1)} %copy-done.35) | copy-start | bytes 772
  521.8 44.0 %copy-start.38 = (pred[256]{0:T(512)(128)(4,1)S(1)}, pred[256]{0:T(512)(128)(4,1)}, u32[]{:S(2)}) copy-start(pred[256]{0:T(512)(128)(4,1)} %copy-done.37) | copy-start | bytes 772
  521.8 44.0 %copy-start.41 = (pred[128]{0:T(512)(128)(4,1)S(1)}, pred[128]{0:T(512)(128)(4,1)}, u32[]{:S(2)}) copy-start(pred[128]{0:T(512)(128)(4,1)} %get-tuple-element.1003) | copy-start | bytes 388
  556.0 9.8 %collective-permute-start.1 = (bf16[3,256]{1,0:T(4,128)(2,1)S(1)}, bf16[3,256]{1,0:T(4,128)(2,1)S(1)}, u32[]{:S(2)}, u32[]{:S(2)}) collective-permute-start(bf16[3,256]{1,0:T(4,128)(2,1)S(1)} %slice.115), channel_id=1, source_target_pairs={{8,0},{16,8},{24,16},{32,24},{40,32},{48,40},{56,48},{64,56},{72,6... | collective-permute-start | bytes 4616 | tf_op jit(solution)/shard_map/ppermute | solution.py:14
  (9 other events, 9.9 us)
Sparse Core Ops, SparseCore 0:
  89.8 92.4 all-gather.8
  186.3 81.9 all-gather.10
  271.6 81.7 all-gather.12
  357.2 82.2 all-gather.14
  524.2 31.0 reduce-scatter.1
where the time goes:
time: 581 us; the launch traced here: 574 us
  waiting for transfers between devices  367 us (63%)
  matrix products  98.1 us (17%)
  other arithmetic  30.5 us (5%)
  starting transfers between devices  26.2 us (5%)
  blocking collectives  21.1 us (4%)
  between operations  15.6 us (3%)
  local copies, waits for them, and re-layouts  12.1 us (2%)
    all_gather x2, waiting for transfers between devices, prefix(): lax.all_gather(a.astype(kind), axis)  174 us
    all_gather x2, waiting for transfers between devices, prefix_2(): lax.all_gather(part.astype(kind), axis)  161 us
    dot_general x65, matrix products, compose(): jnp.matmul(after_map[0], before_map[1], precision=HIGHEST) + after_map[1]  71 us
    reduce_scatter x1, waiting for transfers between devices, on_device(): lax.psum_scatter(partial_sum.astype(jnp.bfloat16), 'head', scatter_dimens...  30.2 us
    all_gather x1, blocking collectives, on_device(): feature_part = lax.all_gather(delayed, 'head', axis=1, tiled=True)  21.1 us
    another operation x5, other arithmetic, span_terms(): jax.scipy.linalg.solve_triangular(system, stacked, lower=True, unit_diago...  19.9 us
    all_to_all x1, starting transfers between devices, on_device(): lax.all_to_all(loaded.reshape(sources, block_rows, local_width), 'seq', s...  14.8 us
  transfers between devices with their start and end apart: 8, of which 7 were waited for; matrix products, arithmetic and copies ran while one was open for 4% of the time, Pallas kernels for 0%

commit v1 on v0

--- a/solution.py
+++ b/solution.py
@@ -6,6 +6,19 @@
 SPAN = 128
 EPSILON = 1e-06
 HIGHEST = lax.Precision.HIGHEST
+
+
+def ring_gather(array, axis, dim):
+    ways = lax.axis_size(axis)
+    up = [(d, (d + 1) % ways) for d in range(ways)]
+    down = [(d, (d - 1) % ways) for d in range(ways)]
+    earlier, later = ([array], [array])
+    for _ in range(ways // 2):
+        earlier.append(lax.ppermute(earlier[-1], axis, up))
+    for _ in range((ways - 1) // 2):
+        later.append(lax.ppermute(later[-1], axis, down))
+    line = jnp.concatenate([*earlier[::-1], *later[1:]], axis=dim)
+    return jnp.roll(line, (lax.axis_index(axis) - ways // 2) * array.shape[dim], axis=dim)
 
 
 def from_behind(x, axis, by):
@@ -211,7 +224,7 @@
         jnp.zeros((frames, w_value.shape[1]), jnp.float32),
         jnp.zeros((frames, heads_local), jnp.float32),
     )
-    feature_part = lax.all_gather(delayed, "head", axis=1, tiled=True)
+    feature_part = ring_gather(delayed, "head", 1)
     results = []
     for running, weight in zip(empty, (w_query, w_key, w_value, w_beta)):
         results.append(jnp.dot(feature_part, weight, preferred_element_type=jnp.float32))

time: 581 us -> 583 us (level)
  starting transfers between devices: 26.2 us -> 47.9 us
  blocking collectives: 21.1 us -> 0 us
  waiting for transfers between devices: 367 us -> 373 us
    ppermute x0 -> x7, starting transfers between devices: none -> 22.8 us  [the longest x3 13.8 us: ring_gather(): later.append(lax.ppermute(later[-1], axis, down))]
    all_gather x1 -> x0, blocking collectives: 21.1 us -> none  [on_device(): feature_part = lax.all_gather(delayed, 'head', axis=1, tiled=True)]
  transfers between devices with their start and end apart: 8 -> 15, of which waited for: 7 -> 10; matrix products, arithmetic and copies ran while one was open for 4% -> 4% of each run, Pallas kernels for 0% -> 0%
where the time goes in v1:
time: 583 us; the launch traced here: 576 us
  waiting for transfers between devices  373 us (64%)
  matrix products  95.7 us (16%)
  starting transfers between devices  47.9 us (8%)
  other arithmetic  30.5 us (5%)
  between operations  15.6 us (3%)
  local copies, waits for them, and re-layouts  10.9 us (2%)
    all_gather x2, waiting for transfers between devices, prefix(): lax.all_gather(a.astype(kind), axis)  173 us
    all_gather x2, waiting for transfers between devices, prefix_2(): lax.all_gather(part.astype(kind), axis)  161 us
    dot_general x65, matrix products, compose(): jnp.matmul(after_map[0], before_map[1], precision=HIGHEST) + after_map[1]  71.1 us
    reduce_scatter x1, waiting for transfers between devices, on_device(): lax.psum_scatter(partial_sum.astype(jnp.bfloat16), 'head', scatter_dimens...  30.1 us
    another operation x5, other arithmetic, span_terms(): jax.scipy.linalg.solve_triangular(system, stacked, lower=True, unit_diago...  19.9 us
    all_to_all x1, starting transfers between devices, on_device(): lax.all_to_all(loaded.reshape(sources, block_rows, local_width), 'seq', s...  14.8 us
    ppermute x3, starting transfers between devices, ring_gather(): later.append(lax.ppermute(later[-1], axis, down))  13.8 us
  transfers between devices with their start and end apart: 15, of which 10 were waited for; matrix products, arithmetic and copies ran while one was open for 4% of the time, Pallas kernels for 0%

profile of v1, /device:TPU:1, one launch (start us, length us, event | category | flops | bytes accessed | tf_op | source)
XLA Modules:
  0.0 576.3 jit_solution(4453279865362234732)
XLA Ops:
  7.2 1.6 reshape.670
  8.8 14.8 %all-to-all-start = ((bf16[64,2,256]{2,1,0:T(2,128)(2,1)}), bf16[64,2,256]{2,1,0:T(2,128)(2,1)S(1)}, u32[]{:S(2)}, u32[]{:S(2)}) async-start(bf16[64,2,256]{2,1,0:T(2,128)(2,1)} %reshape.670), calls=%async_computation | async-start | bytes 131072 | tf_op jit(solution)/shard_map/all_to_all | solution.py:195
  23.8 2.7 sort.17
  28.1 1.3 select_reduce_fusion.2
  30.6 1.8 fusion.117
  32.6 1.1 all-to-all-done
  34.6 2.4 collective-permute-start
  37.9 3.2 collective-permute-start.1
  41.2 4.2 collective-permute-done.1
  45.4 1.9 collective-permute-start.2
  48.0 4.7 collective-permute-start.5
  52.7 1.9 collective-permute-start.3
  55.3 4.6 collective-permute-start.6
  59.9 1.9 collective-permute-start.4
  61.9 4.6 collective-permute-start.7
  66.6 1.2 collective-permute-done.7
  67.9 1.8 multiply_reduce_fusion.10
  71.6 19.7 %custom-call.10 = f32[2,1,128,128]{2,3,1,0:T(8,128)S(1)} custom-call(f32[2,1,128,128]{3,2,1,0:T(8,128)S(1)} %add_bitcast_fusion), custom_call_target="InvertDiagBlocksLowerTriangular" | custom-call | tf_op jit(solution)/shard_map/vmap()/while/body/eval_jaxpr/jit(_solve_triangular)/triangular_solve/custom-call.1 | solution.py:98
  94.0 1.6 copy.156
  98.0 87.0 %all-gather.11.cloned.1.call-done = bf16[128,128,128]{2,1,0:T(8,128)(2,1)} async-done(((bf16[2,128,128]{2,1,0:T(8,128)(2,1)}), bf16[128,128,128]{2,1,0:T(8,128)(2,1)}) %all-gather.11.cloned.1.call-update) | async-done | bytes 4194320 | tf_op jit(solution)/shard_map/all_gather | solution.py:33
  185.0 85.9 %all-gather.9.cloned.1.call-done = bf16[128,128,128]{2,1,0:T(8,128)(2,1)} async-done(((bf16[2,128,128]{2,1,0:T(8,128)(2,1)}), bf16[128,128,128]{2,1,0:T(8,128)(2,1)}) %all-gather.9.cloned.1.call-update) | async-done | bytes 4194320 | tf_op jit(solution)/shard_map/all_gather | solution.py:33
  270.9 1.1 while.25
  278.3 1.1 fusion.70
  281.4 74.8 %all-gather.13.cloned.1.call-done = bf16[128,128,128]{2,1,0:T(8,128)(2,1)} async-done(((bf16[2,128,128]{2,1,0:T(8,128)(2,1)}), bf16[128,128,128]{2,1,0:T(8,128)(2,1)}) %all-gather.13.cloned.1.call-update) | async-done | bytes 4194320 | tf_op jit(solution)/shard_map/all_gather | solution.py:53
  356.3 85.7 %all-gather.15.cloned.1.call-done = bf16[128,128,128]{2,1,0:T(8,128)(2,1)} async-done(((bf16[2,128,128]{2,1,0:T(8,128)(2,1)}), bf16[128,128,128]{2,1,0:T(8,128)(2,1)}) %all-gather.15.cloned.1.call-update) | async-done | bytes 4194320 | tf_op jit(solution)/shard_map/all_gather | solution.py:53
  442.0 73.4 %while.26 = (s32[]{:T(128)}, f32[2,128,128]{2,1,0:T(8,128)S(1)}, s32[]{:T(128)}, bf16[64,2,128,128]{3,2,1,0:T(8,128)(2,1)}, bf16[64,2,128,128]{3,2,1,0:T(8,128)(...) while((s32[]{:T(128)}, f32[2,128,128]{2,1,0:T(8,128)S(1)}, s32[]{:T(128)}, ...), condition=%wide.region_16.19_spmd.clone, body=%wide.region_15.18_spmd.clone.sunk | while | flops 50495496 | bytes 789157 | solution.py:69
  442.0 1.1 fusion.171
  446.6 1.1 fusion.171
  450.0 1.1 fusion.171
  453.5 1.1 fusion.171
  456.9 1.1 fusion.171
  460.4 1.1 fusion.171
  463.8 1.1 fusion.171
  467.3 1.1 fusion.171
  470.7 1.1 fusion.171
  474.1 1.1 fusion.171
  477.6 1.1 fusion.171
  481.0 1.1 fusion.171
  487.9 1.1 fusion.171
  494.8 1.1 fusion.171
  501.7 1.1 fusion.171
  516.4 1.4 convolution_add_fusion.8
  519.6 1.7 multiply_reduce_fusion.1
  525.3 1.2 fusion.11
  527.6 30.1 %reduce-scatter.2.cloned.1.call-done = bf16[128,256]{1,0:T(8,128)(2,1)} async-done(((bf16[128,2048]{1,0:T(8,128)(2,1)}), bf16[128,256]{1,0:T(8,128)(2,1)}) %reduce-scatter.2.cloned.1.call-update) | async-done | bytes 65552 | tf_op jit(solution)/shard_map/reduce_scatter | solution.py:292
  558.3 7.5 %collective-permute-start.8 = (bf16[3,256]{1,0:T(4,128)(2,1)S(1)}, bf16[3,256]{1,0:T(4,128)(2,1)S(1)}, u32[]{:S(2)}, u32[]{:S(2)}) collective-permute-start(bf16[3,256]{1,0:T(4,128)(2,1)S(1)} %slice.115), channel_id=1, source_target_pairs={{8,0},{16,8},{24,16},{32,24},{40,32},{48,40},{56,48},{64,56},{72,6... | collective-permute-start | bytes 4616 | tf_op jit(solution)/shard_map/ppermute | solution.py:27
  566.7 1.5 collective-permute-done.8
  568.2 1.6 and_select_fusion.3
  (300 shorter events, 85.1 us)
Async XLA Ops:
  7.2 89.4 %copy-start = (bf16[2048,256]{1,0:T(8,128)(2,1)S(1)}, bf16[2048,256]{1,0:T(8,128)(2,1)}, u32[]{:S(2)}) copy-start(bf16[2048,256]{1,0:T(8,128)(2,1)} %param.23) | copy-start | bytes 3145732
  7.2 64.0 %copy-start.19 = (f32[2]{0:T(128)S(1)}, f32[2]{0:T(128)}, u32[]{:S(2)}) copy-start(f32[2]{0:T(128)} %param.27) | copy-start | bytes 28
  7.2 64.0 %copy-start.17 = (bf16[2048,2]{0,1:T(2,128)(2,1)S(1)}, bf16[2048,2]{0,1:T(2,128)(2,1)}, u32[]{:S(2)}) copy-start(bf16[2048,2]{0,1:T(2,128)(2,1)} %param.26) | copy-start | bytes 24580
  8.8 24.9 %all-to-all-start = ((bf16[64,2,256]{2,1,0:T(2,128)(2,1)}), bf16[64,2,256]{2,1,0:T(2,128)(2,1)S(1)}, u32[]{:S(2)}, u32[]{:S(2)}) async-start(bf16[64,2,256]{2,1,0:T(2,128)(2,1)} %reshape.670), calls=%async_computation | async-start | bytes 131072 | tf_op jit(solution)/shard_map/all_to_all | solution.py:195
  23.6 161.3 %all-gather.11.cloned.1.call-start = ((), (), s32[]{:S(2)}) async-start(), calls=%async_computation.4 | async-start | bytes 4259840 | tf_op jit(solution)/shard_map/all_gather | solution.py:33
  34.6 3.2 collective-permute-start
  37.9 7.5 %collective-permute-start.1 = (bf16[128,256]{1,0:T(8,128)(2,1)S(1)}, bf16[128,256]{1,0:T(8,128)(2,1)S(1)}, u32[]{:S(2)}, u32[]{:S(2)}) collective-permute-start(bf16[128,256]{1,0:T(8,128)(2,1)S(1)} %and_select_fusion.7), channel_id=1, source_target_pairs={{0,1},{1,2},{2,3},{3,4},{4,5},{5,6},{6,7},{7,0},{8,9},{9,10},{10,1... | collective-permute-start | bytes 196616 | tf_op jit(solution)/shard_map/ppermute | solution.py:17
  45.4 7.3 %collective-permute-start.2 = (bf16[128,256]{1,0:T(8,128)(2,1)S(1)}, bf16[128,256]{1,0:T(8,128)(2,1)S(1)}, u32[]{:S(2)}, u32[]{:S(2)}) collective-permute-start(bf16[128,256]{1,0:T(8,128)(2,1)S(1)} %collective-permute-done.1), channel_id=1, source_target_pairs={{0,1},{1,2},{2,3},{3,4},{4,5},{5,6},{6,7},{7,0},{8,9},{9,10},{10,1... | collective-permute-start | bytes 196616 | tf_op jit(solution)/shard_map/ppermute | solution.py:17
  48.0 22.6 %copy-start.1 = (bf16[2048,256]{1,0:T(8,128)(2,1)S(1)}, bf16[2048,256]{1,0:T(8,128)(2,1)}, u32[]{:S(2)}) copy-start(bf16[2048,256]{1,0:T(8,128)(2,1)} %param.25) | copy-start | bytes 3145732
  48.0 7.3 %collective-permute-start.5 = (bf16[128,256]{1,0:T(8,128)(2,1)S(1)}, bf16[128,256]{1,0:T(8,128)(2,1)S(1)}, u32[]{:S(2)}, u32[]{:S(2)}) collective-permute-start(bf16[128,256]{1,0:T(8,128)(2,1)S(1)} %and_select_fusion.7), channel_id=1, source_target_pairs={{0,7},{1,0},{2,1},{3,2},{4,3},{5,4},{6,5},{7,6},{8,15},{9,8},{10,9... | collective-permute-start | bytes 196616 | tf_op jit(solution)/shard_map/ppermute | solution.py:19
  52.7 7.2 %collective-permute-start.3 = (bf16[128,256]{1,0:T(8,128)(2,1)S(1)}, bf16[128,256]{1,0:T(8,128)(2,1)S(1)}, u32[]{:S(2)}, u32[]{:S(2)}) collective-permute-start(bf16[128,256]{1,0:T(8,128)(2,1)S(1)} %collective-permute-done.2), channel_id=1, source_target_pairs={{0,1},{1,2},{2,3},{3,4},{4,5},{5,6},{6,7},{7,0},{8,9},{9,10},{10,1... | collective-permute-start | bytes 196616 | tf_op jit(solution)/shard_map/ppermute | solution.py:17
  55.3 6.5 %collective-permute-start.6 = (bf16[128,256]{1,0:T(8,128)(2,1)S(1)}, bf16[128,256]{1,0:T(8,128)(2,1)S(1)}, u32[]{:S(2)}, u32[]{:S(2)}) collective-permute-start(bf16[128,256]{1,0:T(8,128)(2,1)S(1)} %collective-permute-done.5), channel_id=1, source_target_pairs={{0,7},{1,0},{2,1},{3,2},{4,3},{5,4},{6,5},{7,6},{8,15},{9,8},{10,9... | collective-permute-start | bytes 196616 | tf_op jit(solution)/shard_map/ppermute | solution.py:19
  59.9 6.5 %collective-permute-start.4 = (bf16[128,256]{1,0:T(8,128)(2,1)S(1)}, bf16[128,256]{1,0:T(8,128)(2,1)S(1)}, u32[]{:S(2)}, u32[]{:S(2)}) collective-permute-start(bf16[128,256]{1,0:T(8,128)(2,1)S(1)} %collective-permute-done.3), channel_id=1, source_target_pairs={{0,1},{1,2},{2,3},{3,4},{4,5},{5,6},{6,7},{7,0},{8,9},{9,10},{10,1... | collective-permute-start | bytes 196616 | tf_op jit(solution)/shard_map/ppermute | solution.py:17
  61.9 5.9 %collective-permute-start.7 = (bf16[128,256]{1,0:T(8,128)(2,1)S(1)}, bf16[128,256]{1,0:T(8,128)(2,1)S(1)}, u32[]{:S(2)}, u32[]{:S(2)}) collective-permute-start(bf16[128,256]{1,0:T(8,128)(2,1)S(1)} %collective-permute-done.6), channel_id=1, source_target_pairs={{0,7},{1,0},{2,1},{3,2},{4,3},{5,4},{6,5},{7,6},{8,15},{9,8},{10,9... | collective-permute-start | bytes 196616 | tf_op jit(solution)/shard_map/ppermute | solution.py:19
  67.8 28.4 %copy-start.16 = (bf16[128,256]{1,0:T(8,128)(2,1)S(1)}, bf16[128,256]{1,0:T(8,128)(2,1)}, u32[]{:S(2)}) copy-start(bf16[128,256]{1,0:T(8,128)(2,1)} %param.22) | copy-start | bytes 196612
  67.9 28.7 %copy-start.18 = (f32[128]{0:T(128)S(1)}, f32[128]{0:T(128)}, u32[]{:S(2)}) copy-start(f32[128]{0:T(128)} %param.28) | copy-start | bytes 1540
  70.6 0.9 copy-start.13
  70.7 27.3 %copy-start.5 = (f32[2,128,128]{1,2,0:T(8,128)}, f32[2,128,128]{1,2,0:T(8,128)S(1)}, u32[]{:S(2)}) copy-start(f32[2,128,128]{1,2,0:T(8,128)S(1)} %bitcast_divide_fusion.4) | copy-start | bytes 393220
  71.2 25.3 %copy-start.4 = (f32[128,256]{0,1:T(8,128)}, f32[128,256]{0,1:T(8,128)S(1)}, u32[]{:S(2)}) copy-start(f32[128,256]{0,1:T(8,128)S(1)} %fusion.30) | copy-start | bytes 393220
  93.2 177.7 %all-gather.9.cloned.1.call-start = ((), (), s32[]{:S(2)}) async-start(), calls=%async_computation.3 | async-start | bytes 4259840 | tf_op jit(solution)/shard_map/all_gather | solution.py:33
  94.0 262.3 %all-gather.13.cloned.1.call-start = ((), (), s32[]{:S(2)}) async-start(), calls=%async_computation.5 | async-start | bytes 4259840 | tf_op jit(solution)/shard_map/all_gather | solution.py:53
  95.6 346.4 %all-gather.15.cloned.1.call-start = ((), (), s32[]{:S(2)}) async-start(), calls=%async_computation.6 | async-start | bytes 4259840 | tf_op jit(solution)/shard_map/all_gather | solution.py:53
  96.6 180.4 %copy-start.24 = (f32[128]{0:T(128)}, f32[128]{0:T(128)S(1)}, u32[]{:S(2)}) copy-start(f32[128]{0:T(128)S(1)} %broadcast_multiply_fusion.3) | copy-start | bytes 1540
  98.0 178.1 %copy-start.15 = (f32[2,128,128]{2,1,0:T(8,128)}, f32[2,128,128]{2,1,0:T(8,128)S(1)}, u32[]{:S(2)}) copy-start(f32[2,128,128]{2,1,0:T(8,128)S(1)} %fusion.25) | copy-start | bytes 393220
  273.3 4.9 copy-start.23
  275.3 282.4 %reduce-scatter.2.cloned.1.call-start = ((), (), s32[]{:S(2)}) async-start(), calls=%async_computation.2 | async-start | bytes 589824 | tf_op jit(solution)/shard_map/reduce_scatter | solution.py:292
  276.9 4.0 copy-start.7
  277.4 0.9 copy-start.10
  279.8 1.1 copy-start.6
  515.4 5.9 %copy-start.8 = (f32[2,128,128]{2,1,0:T(8,128)S(1)}, f32[2,128,128]{2,1,0:T(8,128)}, u32[]{:S(2)}) copy-start(f32[2,128,128]{2,1,0:T(8,128)} %copy-done.7) | copy-start | bytes 393220
  515.4 5.9 %copy-start.9 = (f32[2,128,128]{1,2,0:T(8,128)S(1)}, f32[2,128,128]{1,2,0:T(8,128)}, u32[]{:S(2)}) copy-start(f32[2,128,128]{1,2,0:T(8,128)} %fusion.70) | copy-start | bytes 393220
  515.5 6.2 %copy-start.11 = (f32[2,128,128]{2,1,0:T(8,128)S(1)}, f32[2,128,128]{2,1,0:T(8,128)}, u32[]{:S(2)}) copy-start(f32[2,128,128]{2,1,0:T(8,128)} %copy-done.10) | copy-start | bytes 393220
  515.5 6.5 %copy-start.12 = (f32[2,128,128]{1,2,0:T(8,128)S(1)}, f32[2,128,128]{1,2,0:T(8,128)}, u32[]{:S(2)}) copy-start(f32[2,128,128]{1,2,0:T(8,128)} %fusion.39) | copy-start | bytes 393220
  515.5 6.5 %copy-start.14 = (f32[2,128,128]{2,1,0:T(8,128)S(1)}, f32[2,128,128]{2,1,0:T(8,128)}, u32[]{:S(2)}) copy-start(f32[2,128,128]{2,1,0:T(8,128)} %copy-done.13) | copy-start | bytes 393220
  516.4 7.5 %copy-start.22 = (f32[2,128]{1,0:T(2,128)S(1)}, f32[2,128]{1,0:T(2,128)}, u32[]{:S(2)}) copy-start(f32[2,128]{1,0:T(2,128)} %get-tuple-element.988) | copy-start | bytes 3076
  518.2 6.1 %copy-start.3 = (bf16[2048,256]{1,0:T(8,128)(2,1)S(1)}, bf16[2048,256]{1,0:T(8,128)(2,1)}, u32[]{:S(2)}) copy-start(bf16[2048,256]{1,0:T(8,128)(2,1)} %param.24) | copy-start | bytes 3145732
  521.3 3.5 copy-start.2
  523.3 2.0 copy-start.20
  524.3 2.3 copy-start.27
  524.3 2.3 copy-start.26
  524.3 2.3 copy-start.25
  524.3 43.9 %copy-start.21 = (pred[128]{0:T(512)(128)(4,1)S(1)}, pred[128]{0:T(512)(128)(4,1)}, u32[]{:S(2)}) copy-start(pred[128]{0:T(512)(128)(4,1)} %get-tuple-element.1003) | copy-start | bytes 388
  558.3 9.8 %collective-permute-start.8 = (bf16[3,256]{1,0:T(4,128)(2,1)S(1)}, bf16[3,256]{1,0:T(4,128)(2,1)S(1)}, u32[]{:S(2)}, u32[]{:S(2)}) collective-permute-start(bf16[3,256]{1,0:T(4,128)(2,1)S(1)} %slice.115), channel_id=1, source_target_pairs={{8,0},{16,8},{24,16},{32,24},{40,32},{48,40},{56,48},{64,56},{72,6... | collective-permute-start | bytes 4616 | tf_op jit(solution)/shard_map/ppermute | solution.py:27
Sparse Core Ops, SparseCore 0:
  93.3 91.5 all-gather.10
  188.9 81.9 all-gather.8
  274.2 82.0 all-gather.12
  360.1 81.8 all-gather.14
  526.7 30.9 reduce-scatter.1
